TPU v7x, 128 devices: a whole 4x4x4 slice. The times are simulated.
128 devices in a mesh: pop: 4 (over y_hi, core), tp: 16 (over z, x), pp: 2 (over y_lo).
Axes of the slice: x: 4, y: 4 (y_hi: 2, y_lo: 2; y = y_hi * 2 + y_lo), z: 4, core: 2. Of those that a mesh axis runs over, the one named last changes fastest.
Arguments:
- hidden_in: bfloat16 [256, 8, 4096], P('tp', 'pop'), may hold values from -6 to 6
- norm_gain: float32 [2, 4096], P('pp'), may hold values from 0.5 to 1.5
- w_gate: bfloat16 [2, 4096, 12288], P('pp', None, 'tp'), may hold values from -0.09375 to 0.09375
- w_up: bfloat16 [2, 4096, 12288], P('pp', None, 'tp'), may hold values from -0.09375 to 0.09375
- w_down: bfloat16 [2, 12288, 4096], P('pp', 'tp'), may hold values from -0.0546875 to 0.0546875
- gate_left: bfloat16 [2, 8, 4096], P('pp', 'pop'), may hold values from -6 to 6
- gate_right: bfloat16 [2, 8, 12288], P('pp', 'pop', 'tp'), may hold values from -6 to 6
- up_left: bfloat16 [2, 8, 4096], P('pp', 'pop'), may hold values from -6 to 6
- up_right: bfloat16 [2, 8, 12288], P('pp', 'pop', 'tp'), may hold values from -6 to 6
- down_left: bfloat16 [2, 8, 12288], P('pp', 'pop', 'tp'), may hold values from -6 to 6
- down_right: bfloat16 [2, 8, 4096], P('pp', 'pop'), may hold values from -6 to 6
- ranks: int32 [8], P('pop'), may hold values from 0 to 7, each once
Outputs:
- section_out: bfloat16 [2, 256, 8, 4096], P('pp', 'tp', 'pop')
- update_gate: bfloat16 [2, 4096, 12288], P('pp', 'pop', 'tp')
- update_up: bfloat16 [2, 4096, 12288], P('pp', 'pop', 'tp')
- update_down: bfloat16 [2, 12288, 4096], P('pp', 'tp', 'pop')
Inputs may be any that keep to these rules, and one draw needn't show every extreme that they name: `ranks`: each number from 0 to 7 is the rank of exactly one member.
All inputs are finite; a program needn't handle non-finite values.
Results may differ from a plain program's by a relative error of at most 0.014.
Values may be sent and summed in bfloat16 or wider, within the bound.
No kernel may reach another device: no remote copies, remote signals or barrier semaphores. Data moves between devices by JAX's collectives and lax.ppermute only.
A program may use at most 128 MiB of HBM per device.

v0:
```python
import math
import jax
import jax.numpy as jnp
from jax import lax
from jax.sharding import PartitionSpec as P

sigma_scale = 0.3
norm_eps = 1e-05


def from_behind(block, axis, distance):
    devices = range(lax.axis_size(axis))
    route = [(i - distance, i) for i in devices if i - distance in devices]
    return lax.ppermute(block, axis, route)


def sent_together(arrays, axis, dim, along):
    both = jnp.concatenate(arrays, axis=along)
    out, at, done = (lax.all_gather(both, axis, axis=dim, tiled=True), 0, [])
    for a in arrays:
        done.append(lax.slice_in_dim(out, at, at + a.shape[along], axis=along))
        at += a.shape[along]
    return tuple(done)


def feed_forward(
    block,
    gain,
    w_gate,
    w_up,
    w_down,
    gate_left,
    gate_right,
    up_left,
    up_right,
    down_left,
    down_right,
):
    values = block.astype(jnp.float32)
    mean_sq = jnp.mean(values * values, axis=-1, keepdims=True)
    normed = (values * lax.rsqrt(mean_sq + norm_eps) * gain).astype(jnp.bfloat16)
    coef_in = sigma_scale / math.sqrt(block.shape[-1])
    coef_hidden = sigma_scale / math.sqrt(w_gate.shape[-1] * lax.axis_size("tp"))
    gate_wide = gate_right.astype(jnp.float32)[None]
    up_wide = up_right.astype(jnp.float32)[None]
    down_wide = down_right.astype(jnp.float32)[None]
    piece = lax.all_gather(normed, "tp", axis=0, tiled=True)
    gate = jnp.einsum("rkd,df->rkf", piece, w_gate, preferred_element_type=jnp.float32)
    gate_side = jnp.einsum("rkd,kd->rk", piece, gate_left, preferred_element_type=jnp.float32)
    gate = gate + coef_in * gate_side[:, :, None] * gate_wide
    upper = jnp.einsum("rkd,df->rkf", piece, w_up, preferred_element_type=jnp.float32)
    up_side = jnp.einsum("rkd,kd->rk", piece, up_left, preferred_element_type=jnp.float32)
    upper = upper + coef_in * up_side[:, :, None] * up_wide
    inner = (jax.nn.silu(gate) * upper).astype(jnp.bfloat16)
    term = jnp.einsum("rkf,fd->rkd", inner, w_down, preferred_element_type=jnp.float32)
    down_side = jnp.einsum("rkf,kf->rk", inner, down_left, preferred_element_type=jnp.float32)
    summed = lax.psum_scatter(
        (term + coef_hidden * down_side[:, :, None] * down_wide).astype(jnp.bfloat16),
        "tp",
        scatter_dimension=0,
        tiled=True,
    ).astype(jnp.float32)
    return (values + summed).astype(jnp.bfloat16)


def grouped_outer(fitness, left, right, groups):
    weighted = (fitness[:, None] * left.astype(jnp.float32)).reshape(groups, -1, left.shape[1])
    other = right.astype(jnp.float32).reshape(groups, -1, right.shape[1])
    parts = jnp.einsum("gmi,gmj->gij", weighted, other)
    rounded = lax.optimization_barrier(parts.astype(jnp.bfloat16)).astype(jnp.float32)
    return jnp.sum(rounded, axis=0)


def per_device(
    hidden_in,
    norm_gain,
    w_gate,
    w_up,
    w_down,
    gate_left,
    gate_right,
    up_left,
    up_right,
    down_left,
    down_right,
    ranks,
):
    seq_rows, members, width = hidden_in.shape
    sections = lax.axis_size("pp")
    section_index = lax.axis_index("pp")
    gain = norm_gain[0]
    gate_weight = w_gate[0]
    up_weight = w_up[0]
    down_weight = w_down[0]
    vectors = [gate_left[0], gate_right[0], up_left[0], up_right[0], down_left[0], down_right[0]]
    block_list = [(0, 0)]
    block_count = len(block_list)
    ticks = block_count + sections - 1
    output = jnp.zeros_like(hidden_in)
    arrived = jnp.zeros((seq_rows, members, width), jnp.bfloat16)
    for tick in range(ticks):
        if tick < block_count:
            own = hidden_in
        else:
            own = jnp.zeros_like(arrived)
        current = jnp.where(section_index == 0, own, arrived)
        position = tick - section_index
        picked = [vector for vector in vectors]
        result = feed_forward(
            current,
            gain,
            gate_weight,
            up_weight,
            down_weight,
            picked[0],
            picked[1],
            picked[2],
            picked[3],
            picked[4],
            picked[5],
        )
        valid = (position >= 0) & (position < block_count)
        before = output
        output = jnp.where(valid, result, before)
        if tick + 1 < ticks:
            arrived = from_behind(result, "pp", 1)
    pop_size = lax.axis_size("pop")
    population = members * pop_size
    all_ranks, all_gl, all_gr, all_ul, all_ur, all_dl, all_dr = (
        lax.all_gather(ranks, "pop", axis=0, tiled=True),
        *sent_together(
            (vectors[0], vectors[1], vectors[2], vectors[3], vectors[4], vectors[5]), "pop", 0, 1
        ),
    )
    fitness = (2.0 * all_ranks.astype(jnp.float32) / (population - 1) - 1.0) / math.sqrt(population)
    row_share = width // pop_size
    row_start = lax.axis_index("pop") * row_share
    own_gl = lax.dynamic_slice_in_dim(all_gl, row_start, row_share, 1)
    own_ul = lax.dynamic_slice_in_dim(all_ul, row_start, row_share, 1)
    own_dr = lax.dynamic_slice_in_dim(all_dr, row_start, row_share, 1)
    sum_gate = grouped_outer(fitness, own_gl, all_gr, pop_size)
    sum_up = grouped_outer(fitness, own_ul, all_ur, pop_size)
    sum_down = grouped_outer(fitness, all_dl, own_dr, pop_size)
    update_gate = sum_gate.astype(jnp.bfloat16)[None]
    update_up = sum_up.astype(jnp.bfloat16)[None]
    update_down = sum_down.astype(jnp.bfloat16)[None]
    return (output[None], update_gate, update_up, update_down)


def solution(mesh):
    placed = (
        P("tp", "pop", None),
        P("pp", None),
        P("pp", None, "tp"),
        P("pp", None, "tp"),
        P("pp", "tp", None),
        P("pp", "pop", None),
        P("pp", "pop", "tp"),
        P("pp", "pop", None),
        P("pp", "pop", "tp"),
        P("pp", "pop", "tp"),
        P("pp", "pop", None),
        P("pop"),
    )
    return jax.shard_map(
        per_device,
        mesh=mesh,
        in_specs=placed,
        out_specs=(
            P("pp", "tp", "pop", None),
            P("pp", "pop", "tp"),
            P("pp", "pop", "tp"),
            P("pp", "tp", "pop"),
        ),
        check_vma=False,
    )
```

profile of v0, /device:TPU:0, one launch (start us, length us, event | category | flops | bytes accessed | tf_op | source)
XLA Modules:
  0.0 329.0 jit_solution(4825222965416994438)
XLA Ops:
  7.2 0.0 copy-start.3
  7.2 0.0 all-gather.4.cloned.1.call-start
  7.2 1.3 fusion.20
  8.6 1.9 fusion.22
  10.4 0.0 all-gather.4.cloned.1.call-update
  10.5 0.0 reduce-scatter.3.cloned.1.call-start
  10.5 0.7 bitcast_convert_fusion.1
  11.2 0.7 bitcast_convert_fusion
  12.0 53.0 %all-gather.4.cloned.1.call-done = bf16[256,2,4096]{2,0,1:T(8,128)(2,1)} async-done(((bf16[16,2,4096]{2,0,1:T(8,128)(2,1)}), bf16[256,2,4096]{2,0,1:T(8,128)(2,1)}) %all-gather.4.cloned.1.call-update) | async-done | bytes 4194320 | tf_op jit(solution)/shard_map/all_gather | solution.py:47
  64.9 3.5 %fusion.32 = f32[2,1,256]{2,1,0:T(1,128)S(1)} fusion(bf16[256,2,4096]{2,0,1:T(8,128)(2,1)} %all-gather.4.cloned.1.call-done, bf16[2,4096,1]{1,0,2:T(2,128)(2,1)} %bitcast.111), kind=kOutput, calls=%fused_computation.41 | convolution fusion | flops 4194304 | bytes 4212736 | tf_op jit(solution)/shard_map/rkd,kd->rk/dot_general | solution.py:52
  68.4 0.0 copy-done
  68.5 0.0 slice-start
  68.5 1.2 fusion.36
  69.7 0.0 slice-start.4
  69.7 5.6 %fusion.6 = f32[256,2,768]{2,0,1:T(8,128)S(1)} fusion(bf16[256,2,4096]{2,0,1:T(8,128)(2,1)S(1)} %copy-done, bf16[1,4096,768]{2,1,0:T(8,128)(2,1)} %param.15), kind=kOutput, calls=%fused_computation.8 | convolution fusion | flops 3221225472 | bytes 12058624 | tf_op jit(solution)/shard_map/rkd,df->rkf/dot_general | solution.py:51
  75.4 0.0 copy-start.5
  75.4 0.0 slice-start.5
  75.4 3.6 %multiply_convert_fusion.1 = bf16[256,2,768]{2,0,1:T(8,128)(2,1)S(1)} fusion(f32[256,2,768]{2,0,1:T(8,128)S(1)} %fusion.6, bf16[256,2,4096]{2,0,1:T(8,128)(2,1)S(1)} %copy-done, bf16[1,4096,768]{2,1,0:T(8,128)(2,1)S(1)} %bitcast.119, f32[2,768]{1,0:T(2,128)S(1)} %get-tuple-element.20, f32[256,2]{0,1:T(2,128)S(1)} %get-tuple-element.22, ...), kind=kOutput, calls=%fused_computation.18 | convolution fusion | flops 3225157632 | bytes 12861440 | tf_op jit(solution)/shard_map/rkd,df->rkf/dot_general | solution.py:48
  79.0 0.3 fusion.40
  79.4 0.0 slice-done.5
  79.4 5.0 %add_convert_fusion.1 = bf16[256,2,4096]{2,0,1:T(8,128)(2,1)} fusion(bf16[256,2,768]{2,0,1:T(8,128)(2,1)S(1)} %multiply_convert_fusion.1, bf16[1,768,4096]{2,1,0:T(8,128)(2,1)S(1)} %bitcast.123, f32[2,4096]{1,0:T(2,128)S(1)} %bitcast_convert_fusion, f32[256,2]{0,1:T(2,128)S(1)} %fusion.45), kind=kOutput, calls=%fused_computation.1 | convolution fusion | flops 3227516928 | bytes 11307008 | tf_op jit(solution)/shard_map/rkf,fd->rkd/dot_general | solution.py:55
  84.4 0.0 reduce-scatter.3.cloned.1.call-update
  84.5 0.0 all-gather.6.cloned.1.call-start
  84.5 77.5 %reduce-scatter.3.cloned.1.call-done = bf16[16,2,4096]{2,0,1:T(8,128)(2,1)} async-done(((bf16[256,2,4096]{2,0,1:T(8,128)(2,1)}), bf16[16,2,4096]{2,0,1:T(8,128)(2,1)}) %reduce-scatter.3.cloned.1.call-update) | async-done | bytes 262160 | tf_op jit(solution)/shard_map/reduce_scatter | solution.py:57
  162.0 1.1 fusion.23
  163.2 3.4 %collective-permute-start = (bf16[16,2,4096]{2,0,1:T(8,128)(2,1)S(1)}, bf16[16,2,4096]{2,0,1:T(8,128)(2,1)S(1)}, u32[]{:S(2)}, u32[]{:S(2)}) collective-permute-start(bf16[16,2,4096]{2,0,1:T(8,128)(2,1)S(1)} %fusion.23), channel_id=1, source_target_pairs={{0,1},{2,3},{4,5},{6,7},{8,9},{10,11},{12,13},{14,15},{16,17},{18,... | collective-permute-start | bytes 786440 | tf_op jit(solution)/shard_map/ppermute | solution.py:14
  166.5 3.9 %collective-permute-done = bf16[16,2,4096]{2,0,1:T(8,128)(2,1)S(1)} collective-permute-done((bf16[16,2,4096]{2,0,1:T(8,128)(2,1)S(1)}, bf16[16,2,4096]{2,0,1:T(8,128)(2,1)S(1)}, u32[]{:S(2)}, u32[]{:S(2)}) %collective-permute-start) | collective-permute-done | bytes 262176 | tf_op jit(solution)/shard_map/ppermute | solution.py:14
  170.4 0.1 fusion.24
  170.6 0.0 copy-done.6
  170.6 0.8 fusion.26
  171.4 0.0 all-gather.6.cloned.1.call-update
  171.5 0.2 reduce-scatter.5.cloned.1.call-start
  171.7 51.6 %all-gather.6.cloned.1.call-done = bf16[256,2,4096]{2,0,1:T(8,128)(2,1)} async-done(((bf16[16,2,4096]{2,0,1:T(8,128)(2,1)}), bf16[256,2,4096]{2,0,1:T(8,128)(2,1)}) %all-gather.6.cloned.1.call-update) | async-done | bytes 4194320 | tf_op jit(solution)/shard_map/all_gather | solution.py:47
  223.3 0.0 copy-done.4
  223.4 3.5 %fusion.30 = f32[2,1,256]{2,1,0:T(1,128)S(1)} fusion(bf16[256,2,4096]{2,0,1:T(8,128)(2,1)} %all-gather.6.cloned.1.call-done, bf16[2,4096,1]{1,0,2:T(2,128)(2,1)S(1)} %bitcast.112), kind=kOutput, calls=%fused_computation.39 | convolution fusion | flops 4194304 | bytes 4212736 | tf_op jit(solution)/shard_map/rkd,kd->rk/dot_general | solution.py:52
  226.9 0.0 slice-start.2
  226.9 1.2 fusion.34
  228.1 5.6 %fusion.4 = f32[256,2,768]{2,0,1:T(8,128)S(1)} fusion(bf16[256,2,4096]{2,0,1:T(8,128)(2,1)S(1)} %copy-done.1, bf16[1,4096,768]{2,1,0:T(8,128)(2,1)} %param.15), kind=kOutput, calls=%fused_computation.6 | convolution fusion | flops 3221225472 | bytes 12058624 | tf_op jit(solution)/shard_map/rkd,df->rkf/dot_general | solution.py:51
  233.8 0.0 slice-start.7
  233.8 3.6 %multiply_convert_fusion = bf16[256,2,768]{2,0,1:T(8,128)(2,1)S(1)} fusion(f32[256,2,768]{2,0,1:T(8,128)S(1)} %fusion.4, bf16[256,2,4096]{2,0,1:T(8,128)(2,1)S(1)} %copy-done.1, bf16[1,4096,768]{2,1,0:T(8,128)(2,1)S(1)} %bitcast.121, f32[256,2]{0,1:T(2,128)S(1)} %fusion.43, f32[256,2]{0,1:T(2,128)S(1)} %fusion.44, f32[2,768]{1,0:T(2,128)S(1)} %get-tuple-element.20, ...), kind=kOutput, calls=%fused_computation.17 | convolution fusion | flops 3225157632 | bytes 12861440 | tf_op jit(solution)/shard_map/rkd,df->rkf/dot_general | solution.py:48
  237.4 0.3 fusion.38
  237.7 0.0 slice-done.6
  237.7 0.0 slice-done.7
  237.8 5.0 %add_convert_fusion = bf16[256,2,4096]{2,0,1:T(8,128)(2,1)} fusion(bf16[256,2,768]{2,0,1:T(8,128)(2,1)S(1)} %multiply_convert_fusion, bf16[1,768,4096]{2,1,0:T(8,128)(2,1)S(1)} %bitcast.125, f32[256,2]{0,1:T(2,128)S(1)} %fusion.42, f32[2,4096]{1,0:T(2,128)S(1)} %bitcast_convert_fusion), kind=kOutput, calls=%fused_computation | convolution fusion | flops 3227516928 | bytes 11307008 | tf_op jit(solution)/shard_map/rkf,fd->rkd/dot_general | solution.py:55
  242.8 0.0 copy-start.7
  242.8 0.0 reduce-scatter.5.cloned.1.call-update
  242.9 0.6 copy-done.11
  243.5 0.6 dynamic-slice
  244.7 0.2 dynamic-update-slice
  245.0 6.4 %all-reduce = s32[8]{0:T(128)S(1)} all-reduce(s32[8]{0:T(128)S(1)} %dynamic-update-slice), channel_id=1, replica_groups=mesh['pop'=4,'tp'=16,'pp'=2] {'pop'}, use_global_device_ids=true, to_apply=%add | all-reduce | flops 8 | bytes 64
  251.4 0.0 copy-done.8
  251.5 7.4 %all-gather = bf16[4,2,14592]{2,1,0:T(2,128)(2,1)S(1)} all-gather(bf16[1,2,14592]{2,1,0:T(2,128)(2,1)S(1)} %bitcast.113), channel_id=1, replica_groups=mesh['pop'=4,'tp'=16,'pp'=2] {'pop'}, dimensions={0}, use_global_device_ids=true | all-gather | bytes 291840 | tf_op jit(solution)/shard_map/all_gather | solution.py:19
  259.0 0.1 reshape.66
  259.1 0.1 convert_multiply_fusion.4
  259.2 0.1 convert_multiply_fusion.6
  259.4 4.5 %fusion.49 = bf16[4,768,1024]{2,1,0:T(8,128)(2,1)} fusion(bf16[4,2,768]{2,1,0:T(2,128)(2,1)S(1)} %reshape.60, bf16[4,2,1024]{2,1,0:T(2,128)(2,1)S(1)} %reshape.61), kind=kOutput, calls=%fused_computation.78 | convolution fusion | flops 12582912 | bytes 6320128 | tf_op jit(solution)/shard_map/gmi,gmj->gij/dot_general | solution.py:69
  263.8 4.5 %fusion.51 = bf16[4,1024,768]{2,1,0:T(8,128)(2,1)} fusion(bf16[4,2,1024]{2,1,0:T(2,128)(2,1)S(1)} %reshape.56, bf16[4,2,768]{2,1,0:T(2,128)(2,1)S(1)} %reshape.57), kind=kOutput, calls=%fused_computation.80 | convolution fusion | flops 12582912 | bytes 6320128 | tf_op jit(solution)/shard_map/gmi,gmj->gij/dot_general | solution.py:69
  268.3 6.0 %reduce_sum.58 = bf16[768,1024]{1,0:T(8,128)(2,1)} reduce(bf16[4,768,1024]{2,1,0:T(8,128)(2,1)} %fusion.49, bf16[]{:T(256)} %constant.15.clone.1), dimensions={0}, to_apply=%region_6.7 | reduce | flops 2359296 | bytes 7864322 | tf_op jit(solution)/shard_map/reduce_sum | solution.py:71
  274.3 5.4 %reduce_sum.56 = bf16[1024,768]{1,0:T(8,128)(2,1)} reduce(bf16[4,1024,768]{2,1,0:T(8,128)(2,1)} %fusion.51, bf16[]{:T(256)} %constant.15.clone.1), dimensions={0}, to_apply=%region_4.5 | reduce | flops 2359296 | bytes 7864322 | tf_op jit(solution)/shard_map/reduce_sum | solution.py:71
  279.7 4.5 %fusion.50 = bf16[4,1024,768]{2,1,0:T(8,128)(2,1)} fusion(bf16[4,2,1024]{2,1,0:T(2,128)(2,1)S(1)} %reshape.58, bf16[4,2,768]{2,1,0:T(2,128)(2,1)S(1)} %reshape.59), kind=kOutput, calls=%fused_computation.79 | convolution fusion | flops 12582912 | bytes 6320128 | tf_op jit(solution)/shard_map/gmi,gmj->gij/dot_general | solution.py:69
  284.2 5.3 %reduce_sum.57 = bf16[1024,768]{1,0:T(8,128)(2,1)} reduce(bf16[4,1024,768]{2,1,0:T(8,128)(2,1)} %fusion.50, bf16[]{:T(256)} %constant.15.clone.1), dimensions={0}, to_apply=%region_5.6 | reduce | flops 2359296 | bytes 7864322 | tf_op jit(solution)/shard_map/reduce_sum | solution.py:71
  289.5 30.8 %reduce-scatter.5.cloned.1.call-done = bf16[16,2,4096]{2,0,1:T(8,128)(2,1)} async-done(((bf16[256,2,4096]{2,0,1:T(8,128)(2,1)}), bf16[16,2,4096]{2,0,1:T(8,128)(2,1)}) %reduce-scatter.5.cloned.1.call-update) | async-done | bytes 262160 | tf_op jit(solution)/shard_map/reduce_scatter | solution.py:57
  320.4 1.1 fusion.29
  321.5 1.0 copy.19
  (50 shorter events, 0.3 us)
Async XLA Ops:
  7.2 61.3 %copy-start.3 = (bf16[1,2,4096]{2,1,0:T(2,128)(2,1)S(1)}, bf16[1,2,4096]{2,1,0:T(2,128)(2,1)}, u32[]{:S(2)}) copy-start(bf16[1,2,4096]{2,1,0:T(2,128)(2,1)} %param.17) | copy-start | bytes 49156
  7.2 57.8 %all-gather.4.cloned.1.call-start = ((), (), s32[]{:S(2)}) async-start(), calls=%async_computation.2 | async-start | bytes 4456448 | tf_op jit(solution)/shard_map/all_gather | solution.py:47
  10.5 151.6 %reduce-scatter.3.cloned.1.call-start = ((), (), s32[]{:S(2)}) async-start(), calls=%async_computation.3 | async-start | bytes 4456448 | tf_op jit(solution)/shard_map/reduce_scatter | solution.py:57
  64.9 3.5 %copy-start = (bf16[256,2,4096]{2,0,1:T(8,128)(2,1)S(1)}, bf16[256,2,4096]{2,0,1:T(8,128)(2,1)}, u32[]{:S(2)}) copy-start(bf16[256,2,4096]{2,0,1:T(8,128)(2,1)} %all-gather.4.cloned.1.call-done) | copy-start | bytes 12582916
  68.5 6.9 %slice-start = ((s8[6291456]{0:T(1024)(128)(4,1)}), s8[4194304]{0:T(1024)(128)(4,1)S(1)}, s32[]{:S(2)}) async-start(s8[6291456]{0:T(1024)(128)(4,1)} %bitcast.118), calls=%async_computation.6 | async-start | bytes 8388608
  69.7 5.7 %slice-start.1 = ((s8[6291456]{0:T(1024)(128)(4,1)}), s8[2097152]{0:T(1024)(128)(4,1)S(1)}, s32[]{:S(2)}) async-start(s8[6291456]{0:T(1024)(128)(4,1)} %bitcast.118), calls=%async_computation.7 | async-start | bytes 4194304
  69.7 9.7 %slice-start.4 = ((s8[6291456]{0:T(1024)(128)(4,1)}), s8[4194304]{0:T(1024)(128)(4,1)S(1)}, s32[]{:S(2)}) async-start(s8[6291456]{0:T(1024)(128)(4,1)} %bitcast.122), calls=%async_computation.10 | async-start | bytes 8388608
  75.4 3.7 %copy-start.5 = (bf16[1,2,768]{2,1,0:T(2,128)(2,1)S(1)}, bf16[1,2,768]{2,1,0:T(2,128)(2,1)}, u32[]{:S(2)}) copy-start(bf16[1,2,768]{2,1,0:T(2,128)(2,1)} %param.21) | copy-start | bytes 9220
  75.4 4.0 %slice-start.5 = ((s8[6291456]{0:T(1024)(128)(4,1)}), s8[2097152]{0:T(1024)(128)(4,1)S(1)}, s32[]{:S(2)}) async-start(s8[6291456]{0:T(1024)(128)(4,1)} %bitcast.122), calls=%async_computation.11 | async-start | bytes 4194304
  84.4 77.6 %copy-start.2 = (bf16[16,2,4096]{2,1,0:T(2,128)(2,1)S(1)}, bf16[16,2,4096]{2,1,0:T(2,128)(2,1)}, u32[]{:S(2)}) copy-start(bf16[16,2,4096]{2,1,0:T(2,128)(2,1)} %param.12) | copy-start | bytes 786436
  84.4 86.2 %copy-start.6 = (f32[1,4096]{1,0:T(1,128)S(1)}, f32[1,4096]{1,0:T(1,128)}, u32[]{:S(2)}) copy-start(f32[1,4096]{1,0:T(1,128)} %param.13) | copy-start | bytes 49156
  84.4 138.9 %copy-start.4 = (bf16[1,2,4096]{2,1,0:T(2,128)(2,1)S(1)}, bf16[1,2,4096]{2,1,0:T(2,128)(2,1)}, u32[]{:S(2)}) copy-start(bf16[1,2,4096]{2,1,0:T(2,128)(2,1)} %param.19) | copy-start | bytes 49156
  84.5 138.9 %all-gather.6.cloned.1.call-start = ((), (), s32[]{:S(2)}) async-start(), calls=%async_computation.4 | async-start | bytes 4456448 | tf_op jit(solution)/shard_map/all_gather | solution.py:47
  163.2 7.3 %collective-permute-start = (bf16[16,2,4096]{2,0,1:T(8,128)(2,1)S(1)}, bf16[16,2,4096]{2,0,1:T(8,128)(2,1)S(1)}, u32[]{:S(2)}, u32[]{:S(2)}) collective-permute-start(bf16[16,2,4096]{2,0,1:T(8,128)(2,1)S(1)} %fusion.23), channel_id=1, source_target_pairs={{0,1},{2,3},{4,5},{6,7},{8,9},{10,11},{12,13},{14,15},{16,17},{18,... | collective-permute-start | bytes 786440 | tf_op jit(solution)/shard_map/ppermute | solution.py:14
  171.5 148.9 %reduce-scatter.5.cloned.1.call-start = ((), (), s32[]{:S(2)}) async-start(), calls=%async_computation.5 | async-start | bytes 4456448 | tf_op jit(solution)/shard_map/reduce_scatter | solution.py:57
  223.4 3.5 %copy-start.1 = (bf16[256,2,4096]{2,0,1:T(8,128)(2,1)S(1)}, bf16[256,2,4096]{2,0,1:T(8,128)(2,1)}, u32[]{:S(2)}) copy-start(bf16[256,2,4096]{2,0,1:T(8,128)(2,1)} %all-gather.6.cloned.1.call-done) | copy-start | bytes 12582916
  226.9 6.9 %slice-start.2 = ((s8[6291456]{0:T(1024)(128)(4,1)}), s8[4194304]{0:T(1024)(128)(4,1)S(1)}, s32[]{:S(2)}) async-start(s8[6291456]{0:T(1024)(128)(4,1)} %bitcast.120), calls=%async_computation.8 | async-start | bytes 8388608
  228.1 5.7 %slice-start.3 = ((s8[6291456]{0:T(1024)(128)(4,1)}), s8[2097152]{0:T(1024)(128)(4,1)S(1)}, s32[]{:S(2)}) async-start(s8[6291456]{0:T(1024)(128)(4,1)} %bitcast.120), calls=%async_computation.9 | async-start | bytes 4194304
  228.1 9.7 %slice-start.6 = ((s8[6291456]{0:T(1024)(128)(4,1)}), s8[4194304]{0:T(1024)(128)(4,1)S(1)}, s32[]{:S(2)}) async-start(s8[6291456]{0:T(1024)(128)(4,1)} %bitcast.124), calls=%async_computation.12 | async-start | bytes 8388608
  233.8 4.0 %slice-start.7 = ((s8[6291456]{0:T(1024)(128)(4,1)}), s8[2097152]{0:T(1024)(128)(4,1)S(1)}, s32[]{:S(2)}) async-start(s8[6291456]{0:T(1024)(128)(4,1)} %bitcast.124), calls=%async_computation.13 | async-start | bytes 4194304
  242.8 0.7 copy-start.11
  242.8 1.9 copy-start.10
  242.8 8.6 %copy-start.8 = (bf16[1,2,768]{2,1,0:T(2,128)(2,1)S(1)}, bf16[1,2,768]{2,1,0:T(2,128)(2,1)}, u32[]{:S(2)}) copy-start(bf16[1,2,768]{2,1,0:T(2,128)(2,1)} %param.18) | copy-start | bytes 9220
  242.8 8.6 %copy-start.9 = (bf16[1,2,768]{2,1,0:T(2,128)(2,1)S(1)}, bf16[1,2,768]{2,1,0:T(2,128)(2,1)}, u32[]{:S(2)}) copy-start(bf16[1,2,768]{2,1,0:T(2,128)(2,1)} %param.20) | copy-start | bytes 9220
  242.8 8.7 %copy-start.7 = (bf16[1,2,4096]{2,1,0:T(2,128)(2,1)S(1)}, bf16[1,2,4096]{2,1,0:T(2,128)(2,1)}, u32[]{:S(2)}) copy-start(bf16[1,2,4096]{2,1,0:T(2,128)(2,1)} %param.22) | copy-start | bytes 49156
Sparse Core Ops, SparseCore 0:
  10.7 54.1 all-gather.3
  84.6 77.3 reduce-scatter.2
  171.6 51.7 all-gather.5
  243.0 77.3 reduce-scatter.4
where the time goes:
time: 329 us
  waiting for transfers between devices  217 us (66%)
  matrix products  52.1 us (16%)
  other arithmetic  24.7 us (8%)
  between operations  14.8 us (4%)
  blocking collectives  13.9 us (4%)
  starting transfers between devices  3.72 us (1%)
    reduce_scatter x2, waiting for transfers between devices, feed_forward(): lax.psum_scatter((term + coef_hidden * down_side[:, :, None] * down_wide)...  108 us
    all_gather x2, waiting for transfers between devices, feed_forward(): piece = lax.all_gather(normed, 'tp', axis=0, tiled=True)  105 us
    reduce_sum x3, other arithmetic, grouped_outer(): return jnp.sum(rounded, axis=0)  16.7 us
    dot_general x3, matrix products, grouped_outer(): parts = jnp.einsum('gmi,gmj->gij', weighted, other)  13.4 us
    dot_general x2, matrix products, feed_forward(): jnp.einsum('rkd,df->rkf', piece, w_up, preferred_element_type=jnp.float32)  11.3 us
    dot_general x2, matrix products, feed_forward(): jnp.einsum('rkf,fd->rkd', inner, w_down, preferred_element_type=jnp.float32)  10.1 us
    all_gather x1, blocking collectives, sent_together(): out, at, done = (lax.all_gather(both, axis, axis=dim, tiled=True), 0, [])  7.43 us
    dot_general x2, matrix products, feed_forward(): jnp.einsum('rkd,df->rkf', piece, w_gate, preferred_element_type=jnp.float32)  7.28 us
  transfers between devices with their start and end apart: 5, of which 5 were waited for; matrix products, arithmetic and copies ran while one was open for 10% of the time, Pallas kernels for 0%

commit v1 on v0

--- a/solution.py
+++ b/solution.py
@@ -44,7 +44,23 @@
     gate_wide = gate_right.astype(jnp.float32)[None]
     up_wide = up_right.astype(jnp.float32)[None]
     down_wide = down_right.astype(jnp.float32)[None]
-    piece = lax.all_gather(normed, "tp", axis=0, tiled=True)
+    count, place, width_2 = (lax.axis_size("tp"), lax.axis_index("tp"), normed.shape[0])
+    forward = [(i_2, (i_2 + 1) % count) for i_2 in range(count)]
+    backward = [(i_2, (i_2 - 1) % count) for i_2 in range(count)]
+    piece = jnp.zeros((*normed.shape[:0], count * width_2, *normed.shape[0 + 1 :]), normed.dtype)
+    piece = lax.dynamic_update_slice_in_dim(piece, normed, place * width_2, axis=0)
+    from_left = from_right = normed
+    middle = count // 2
+    for step in range(1, middle + 1):
+        from_left = lax.ppermute(from_left, "tp", forward)
+        piece = lax.dynamic_update_slice_in_dim(
+            piece, from_left, (place - step) % count * width_2, axis=0
+        )
+        if step < count - middle:
+            from_right = lax.ppermute(from_right, "tp", backward)
+            piece = lax.dynamic_update_slice_in_dim(
+                piece, from_right, (place + step) % count * width_2, axis=0
+            )
     gate = jnp.einsum("rkd,df->rkf", piece, w_gate, preferred_element_type=jnp.float32)
     gate_side = jnp.einsum("rkd,kd->rk", piece, gate_left, preferred_element_type=jnp.float32)
     gate = gate + coef_in * gate_side[:, :, None] * gate_wide

time: 329 us -> 394 us (1.20); the launches traced: 329 us -> 388 us
  starting transfers between devices: 3.72 us -> 82.1 us
  waiting for transfers between devices: 217 us -> 185 us
  local copies, waits for them, and re-layouts: 2.85 us -> 17.1 us
    all_gather x2 -> x0, waiting for transfers between devices: 105 us -> none  [feed_forward(): piece = lax.all_gather(normed, 'tp', axis=0, tiled=True)]
    ppermute x0 -> x30, starting transfers between devices: none -> 78.6 us  [the longest x14 75.1 us: feed_forward(): from_right = lax.ppermute(from_right, 'tp', backward)]
    ppermute x0 -> x30, waiting for transfers between devices: none -> 78 us  [the longest x16 76.9 us: feed_forward(): from_left = lax.ppermute(from_left, 'tp', forward)]
    dynamic_update_slice x0 -> x30, local copies, waits for them, and re-layouts: none -> 11.2 us  [the longest x16 6 us: feed_forward(): lax.dynamic_update_slice_in_dim(piece, from_left, (place - step) % count...]
    reduce_scatter x2, waiting for transfers between devices: 108 us -> 103 us  [feed_forward(): lax.psum_scatter((term + coef_hidden * down_side[:, :, None] * down_wide)...]
  transfers between devices with their start and end apart: 5 -> 33, of which waited for: 5 -> 22; matrix products, arithmetic and copies ran while one was open for 10% -> 11% of each run, Pallas kernels for 0% -> 0%
where the time goes in v1:
time: 394 us; the launch traced here: 388 us
  waiting for transfers between devices  185 us (47%)
  starting transfers between devices  82.1 us (21%)
  matrix products  52 us (13%)
  other arithmetic  21.9 us (6%)
  local copies, waits for them, and re-layouts  17.1 us (4%)
  between operations  15.7 us (4%)
  blocking collectives  13.5 us (3%)
    reduce_scatter x2, waiting for transfers between devices, feed_forward(): lax.psum_scatter((term + coef_hidden * down_side[:, :, None] * down_wide)...  103 us
    ppermute x16, waiting for transfers between devices, feed_forward(): from_left = lax.ppermute(from_left, 'tp', forward)  76.9 us
    ppermute x14, starting transfers between devices, feed_forward(): from_right = lax.ppermute(from_right, 'tp', backward)  75.1 us
    reduce_sum x3, other arithmetic, grouped_outer(): return jnp.sum(rounded, axis=0)  16.9 us
    dot_general x3, matrix products, grouped_outer(): parts = jnp.einsum('gmi,gmj->gij', weighted, other)  13.5 us
    dot_general x2, matrix products, feed_forward(): jnp.einsum('rkf,fd->rkd', inner, w_down, preferred_element_type=jnp.float32)  10.2 us
    dot_general x2, matrix products, feed_forward(): jnp.einsum('rkd,df->rkf', piece, w_up, preferred_element_type=jnp.float32)  9.53 us
    dot_general x2, matrix products, feed_forward(): jnp.einsum('rkd,df->rkf', piece, w_gate, preferred_element_type=jnp.float32)  8.77 us
  transfers between devices with their start and end apart: 33, of which 22 were waited for; matrix products, arithmetic and copies ran while one was open for 11% of the time, Pallas kernels for 0%

profile of v1, /device:TPU:0, one launch (start us, length us, event | category | flops | bytes accessed | tf_op | source)
XLA Modules:
  0.0 387.7 jit_solution(1927474539770059098)
XLA Ops:
  7.3 1.4 fusion.20
  8.7 2.5 broadcast.92.clone
  11.2 0.9 constant_dynamic-update-slice_fusion.34
  12.1 1.6 collective-permute-start
  13.7 4.7 %collective-permute-start.1 = (bf16[16,2,4096]{2,0,1:T(8,128)(2,1)S(1)}, bf16[16,2,4096]{2,0,1:T(8,128)(2,1)S(1)}, u32[]{:S(2)}, u32[]{:S(2)}) collective-permute-start(bf16[16,2,4096]{2,0,1:T(8,128)(2,1)S(1)} %get-tuple-element.15), channel_id=1, source_target_pairs={{0,30},{2,0},{4,2},{6,4},{8,6},{10,8},{12,10},{14,12},{16,14},{18,... | collective-permute-start | bytes 786440 | tf_op jit(solution)/shard_map/ppermute | solution.py:60
  18.7 6.0 %collective-permute-done = bf16[16,2,4096]{2,0,1:T(8,128)(2,1)S(1)} collective-permute-done((bf16[16,2,4096]{2,0,1:T(8,128)(2,1)S(1)}, bf16[16,2,4096]{2,0,1:T(8,128)(2,1)S(1)}, u32[]{:S(2)}, u32[]{:S(2)}) %collective-permute-start) | collective-permute-done | bytes 262176 | tf_op jit(solution)/shard_map/ppermute | solution.py:55
  24.7 5.3 %collective-permute-start.3 = (bf16[16,2,4096]{2,0,1:T(8,128)(2,1)S(1)}, bf16[16,2,4096]{2,0,1:T(8,128)(2,1)S(1)}, u32[]{:S(2)}, u32[]{:S(2)}) collective-permute-start(bf16[16,2,4096]{2,0,1:T(8,128)(2,1)S(1)} %collective-permute-done.1), channel_id=1, source_target_pairs={{0,30},{2,0},{4,2},{6,4},{8,6},{10,8},{12,10},{14,12},{16,14},{18,... | collective-permute-start | bytes 786440 | tf_op jit(solution)/shard_map/ppermute | solution.py:60
  30.1 0.7 constant_dynamic-update-slice_fusion.33
  30.8 0.7 constant_dynamic-update-slice_fusion.32
  31.5 4.0 %collective-permute-done.2 = bf16[16,2,4096]{2,0,1:T(8,128)(2,1)S(1)} collective-permute-done((bf16[16,2,4096]{2,0,1:T(8,128)(2,1)S(1)}, bf16[16,2,4096]{2,0,1:T(8,128)(2,1)S(1)}, u32[]{:S(2)}, u32[]{:S(2)}) %collective-permute-start.2) | collective-permute-done | bytes 262176 | tf_op jit(solution)/shard_map/ppermute | solution.py:55
  35.5 5.3 %collective-permute-start.5 = (bf16[16,2,4096]{2,0,1:T(8,128)(2,1)S(1)}, bf16[16,2,4096]{2,0,1:T(8,128)(2,1)S(1)}, u32[]{:S(2)}, u32[]{:S(2)}) collective-permute-start(bf16[16,2,4096]{2,0,1:T(8,128)(2,1)S(1)} %collective-permute-done.3), channel_id=1, source_target_pairs={{0,30},{2,0},{4,2},{6,4},{8,6},{10,8},{12,10},{14,12},{16,14},{18,... | collective-permute-start | bytes 786440 | tf_op jit(solution)/shard_map/ppermute | solution.py:60
  42.3 3.1 collective-permute-done.4
  45.4 5.3 %collective-permute-start.7 = (bf16[16,2,4096]{2,0,1:T(8,128)(2,1)S(1)}, bf16[16,2,4096]{2,0,1:T(8,128)(2,1)S(1)}, u32[]{:S(2)}, u32[]{:S(2)}) collective-permute-start(bf16[16,2,4096]{2,0,1:T(8,128)(2,1)S(1)} %collective-permute-done.5), channel_id=1, source_target_pairs={{0,30},{2,0},{4,2},{6,4},{8,6},{10,8},{12,10},{14,12},{16,14},{18,... | collective-permute-start | bytes 786440 | tf_op jit(solution)/shard_map/ppermute | solution.py:60
  52.2 2.9 collective-permute-done.6
  55.1 5.3 %collective-permute-start.9 = (bf16[16,2,4096]{2,0,1:T(8,128)(2,1)S(1)}, bf16[16,2,4096]{2,0,1:T(8,128)(2,1)S(1)}, u32[]{:S(2)}, u32[]{:S(2)}) collective-permute-start(bf16[16,2,4096]{2,0,1:T(8,128)(2,1)S(1)} %collective-permute-done.7), channel_id=1, source_target_pairs={{0,30},{2,0},{4,2},{6,4},{8,6},{10,8},{12,10},{14,12},{16,14},{18,... | collective-permute-start | bytes 786440 | tf_op jit(solution)/shard_map/ppermute | solution.py:60
  61.9 2.9 collective-permute-done.8
  64.8 5.3 %collective-permute-start.11 = (bf16[16,2,4096]{2,0,1:T(8,128)(2,1)S(1)}, bf16[16,2,4096]{2,0,1:T(8,128)(2,1)S(1)}, u32[]{:S(2)}, u32[]{:S(2)}) collective-permute-start(bf16[16,2,4096]{2,0,1:T(8,128)(2,1)S(1)} %collective-permute-done.9), channel_id=1, source_target_pairs={{0,30},{2,0},{4,2},{6,4},{8,6},{10,8},{12,10},{14,12},{16,14},{18,... | collective-permute-start | bytes 786440 | tf_op jit(solution)/shard_map/ppermute | solution.py:60
  71.6 2.9 collective-permute-done.10
  74.5 5.6 %collective-permute-start.13 = (bf16[16,2,4096]{2,0,1:T(8,128)(2,1)S(1)}, bf16[16,2,4096]{2,0,1:T(8,128)(2,1)S(1)}, u32[]{:S(2)}, u32[]{:S(2)}) collective-permute-start(bf16[16,2,4096]{2,0,1:T(8,128)(2,1)S(1)} %collective-permute-done.11), channel_id=1, source_target_pairs={{0,30},{2,0},{4,2},{6,4},{8,6},{10,8},{12,10},{14,12},{16,14},{18,... | collective-permute-start | bytes 786440 | tf_op jit(solution)/shard_map/ppermute | solution.py:60
  80.9 0.7 constant_dynamic-update-slice_fusion.22
  81.6 3.3 collective-permute-done.12
  86.8 8.2 %collective-permute-done.14 = bf16[16,2,4096]{2,0,1:T(8,128)(2,1)S(1)} collective-permute-done((bf16[16,2,4096]{2,0,1:T(8,128)(2,1)S(1)}, bf16[16,2,4096]{2,0,1:T(8,128)(2,1)S(1)}, u32[]{:S(2)}, u32[]{:S(2)}) %collective-permute-start.14) | collective-permute-done | bytes 262176 | tf_op jit(solution)/shard_map/ppermute | solution.py:55
  95.0 0.8 constant_dynamic-update-slice_fusion.19
  95.8 3.5 fusion.32
  99.3 3.5 fusion.36
  102.9 5.4 %fusion.10 = f32[256,2,768]{2,0,1:T(8,128)S(1)} fusion(bf16[256,2,4096]{2,0,1:T(8,128)(2,1)} %constant_dynamic-update-slice_fusion.19, bf16[1,4096,768]{2,1,0:T(8,128)(2,1)S(1)} %bitcast.119), kind=kOutput, calls=%fused_computation.12 | convolution fusion | flops 3221225472 | bytes 12058624 | tf_op jit(solution)/shard_map/rkd,df->rkf/dot_general | solution.py:64
  108.3 5.9 %multiply_convert_fusion.1 = bf16[256,2,768]{2,0,1:T(8,128)(2,1)S(1)} fusion(f32[256,2,768]{2,0,1:T(8,128)S(1)} %fusion.10, bf16[256,2,4096]{2,0,1:T(8,128)(2,1)} %constant_dynamic-update-slice_fusion.19, bf16[1,4096,768]{2,1,0:T(8,128)(2,1)S(1)} %bitcast.123, f32[2,768]{1,0:T(2,128)S(1)} %get-tuple-element.24, f32[256,2]{0,1:T(2,128)S(1)} %get-tuple-element.26, ...), kind=kOutput, calls=%fused_computation.18 | convolution fusion | flops 3225157632 | bytes 12861440 | tf_op jit(solution)/shard_map/rkd,df->rkf/dot_general | solution.py:67
  114.6 5.1 %add_convert_fusion.1 = bf16[256,2,4096]{2,0,1:T(8,128)(2,1)} fusion(bf16[256,2,768]{2,0,1:T(8,128)(2,1)S(1)} %multiply_convert_fusion.1, bf16[1,768,4096]{2,1,0:T(8,128)(2,1)S(1)} %bitcast.127, f32[2,4096]{1,0:T(2,128)S(1)} %bitcast_convert_fusion, f32[256,2]{0,1:T(2,128)S(1)} %fusion.45), kind=kOutput, calls=%fused_computation.1 | convolution fusion | flops 3227516928 | bytes 11307008 | tf_op jit(solution)/shard_map/rkf,fd->rkd/dot_general | solution.py:71
  119.8 74.4 %reduce-scatter.3.cloned.1.call-done = bf16[16,2,4096]{2,0,1:T(8,128)(2,1)} async-done(((bf16[256,2,4096]{2,0,1:T(8,128)(2,1)}), bf16[16,2,4096]{2,0,1:T(8,128)(2,1)}) %reduce-scatter.3.cloned.1.call-update) | async-done | bytes 262160 | tf_op jit(solution)/shard_map/reduce_scatter | solution.py:73
  194.1 1.1 fusion.23
  195.2 3.4 collective-permute-start.15
  198.7 3.9 %collective-permute-done.15 = bf16[16,2,4096]{2,0,1:T(8,128)(2,1)S(1)} collective-permute-done((bf16[16,2,4096]{2,0,1:T(8,128)(2,1)S(1)}, bf16[16,2,4096]{2,0,1:T(8,128)(2,1)S(1)}, u32[]{:S(2)}, u32[]{:S(2)}) %collective-permute-start.15) | collective-permute-done | bytes 262176 | tf_op jit(solution)/shard_map/ppermute | solution.py:14
  203.4 1.3 collective-permute-start.16
  204.7 4.1 %collective-permute-start.17 = (bf16[16,2,4096]{2,0,1:T(8,128)(2,1)S(1)}, bf16[16,2,4096]{2,0,1:T(8,128)(2,1)S(1)}, u32[]{:S(2)}, u32[]{:S(2)}) collective-permute-start(bf16[16,2,4096]{2,0,1:T(8,128)(2,1)S(1)} %get-tuple-element.13), channel_id=1, source_target_pairs={{0,30},{2,0},{4,2},{6,4},{8,6},{10,8},{12,10},{14,12},{16,14},{18,... | collective-permute-start | bytes 786440 | tf_op jit(solution)/shard_map/ppermute | solution.py:60
  208.8 4.3 %collective-permute-done.16 = bf16[16,2,4096]{2,0,1:T(8,128)(2,1)S(1)} collective-permute-done((bf16[16,2,4096]{2,0,1:T(8,128)(2,1)S(1)}, bf16[16,2,4096]{2,0,1:T(8,128)(2,1)S(1)}, u32[]{:S(2)}, u32[]{:S(2)}) %collective-permute-start.16) | collective-permute-done | bytes 262176 | tf_op jit(solution)/shard_map/ppermute | solution.py:55
  213.2 5.4 %collective-permute-start.19 = (bf16[16,2,4096]{2,0,1:T(8,128)(2,1)S(1)}, bf16[16,2,4096]{2,0,1:T(8,128)(2,1)S(1)}, u32[]{:S(2)}, u32[]{:S(2)}) collective-permute-start(bf16[16,2,4096]{2,0,1:T(8,128)(2,1)S(1)} %collective-permute-done.17), channel_id=1, source_target_pairs={{0,30},{2,0},{4,2},{6,4},{8,6},{10,8},{12,10},{14,12},{16,14},{18,... | collective-permute-start | bytes 786440 | tf_op jit(solution)/shard_map/ppermute | solution.py:60
  218.6 4.2 %collective-permute-done.18 = bf16[16,2,4096]{2,0,1:T(8,128)(2,1)S(1)} collective-permute-done((bf16[16,2,4096]{2,0,1:T(8,128)(2,1)S(1)}, bf16[16,2,4096]{2,0,1:T(8,128)(2,1)S(1)}, u32[]{:S(2)}, u32[]{:S(2)}) %collective-permute-start.18) | collective-permute-done | bytes 262176 | tf_op jit(solution)/shard_map/ppermute | solution.py:55
  222.9 5.4 %collective-permute-start.21 = (bf16[16,2,4096]{2,0,1:T(8,128)(2,1)S(1)}, bf16[16,2,4096]{2,0,1:T(8,128)(2,1)S(1)}, u32[]{:S(2)}, u32[]{:S(2)}) collective-permute-start(bf16[16,2,4096]{2,0,1:T(8,128)(2,1)S(1)} %collective-permute-done.19), channel_id=1, source_target_pairs={{0,30},{2,0},{4,2},{6,4},{8,6},{10,8},{12,10},{14,12},{16,14},{18,... | collective-permute-start | bytes 786440 | tf_op jit(solution)/shard_map/ppermute | solution.py:60
  228.3 4.4 %collective-permute-done.20 = bf16[16,2,4096]{2,0,1:T(8,128)(2,1)S(1)} collective-permute-done((bf16[16,2,4096]{2,0,1:T(8,128)(2,1)S(1)}, bf16[16,2,4096]{2,0,1:T(8,128)(2,1)S(1)}, u32[]{:S(2)}, u32[]{:S(2)}) %collective-permute-start.20) | collective-permute-done | bytes 262176 | tf_op jit(solution)/shard_map/ppermute | solution.py:55
  232.7 5.7 %collective-permute-start.23 = (bf16[16,2,4096]{2,0,1:T(8,128)(2,1)S(1)}, bf16[16,2,4096]{2,0,1:T(8,128)(2,1)S(1)}, u32[]{:S(2)}, u32[]{:S(2)}) collective-permute-start(bf16[16,2,4096]{2,0,1:T(8,128)(2,1)S(1)} %collective-permute-done.21), channel_id=1, source_target_pairs={{0,30},{2,0},{4,2},{6,4},{8,6},{10,8},{12,10},{14,12},{16,14},{18,... | collective-permute-start | bytes 786440 | tf_op jit(solution)/shard_map/ppermute | solution.py:60
  238.4 5.0 %collective-permute-done.22 = bf16[16,2,4096]{2,0,1:T(8,128)(2,1)S(1)} collective-permute-done((bf16[16,2,4096]{2,0,1:T(8,128)(2,1)S(1)}, bf16[16,2,4096]{2,0,1:T(8,128)(2,1)S(1)}, u32[]{:S(2)}, u32[]{:S(2)}) %collective-permute-start.22) | collective-permute-done | bytes 262176 | tf_op jit(solution)/shard_map/ppermute | solution.py:55
  243.9 5.8 %collective-permute-start.25 = (bf16[16,2,4096]{2,0,1:T(8,128)(2,1)S(1)}, bf16[16,2,4096]{2,0,1:T(8,128)(2,1)S(1)}, u32[]{:S(2)}, u32[]{:S(2)}) collective-permute-start(bf16[16,2,4096]{2,0,1:T(8,128)(2,1)S(1)} %collective-permute-done.23), channel_id=1, source_target_pairs={{0,30},{2,0},{4,2},{6,4},{8,6},{10,8},{12,10},{14,12},{16,14},{18,... | collective-permute-start | bytes 786440 | tf_op jit(solution)/shard_map/ppermute | solution.py:60
  249.7 6.1 %collective-permute-done.24 = bf16[16,2,4096]{2,0,1:T(8,128)(2,1)S(1)} collective-permute-done((bf16[16,2,4096]{2,0,1:T(8,128)(2,1)S(1)}, bf16[16,2,4096]{2,0,1:T(8,128)(2,1)S(1)}, u32[]{:S(2)}, u32[]{:S(2)}) %collective-permute-start.24) | collective-permute-done | bytes 262176 | tf_op jit(solution)/shard_map/ppermute | solution.py:55
  256.3 5.8 %collective-permute-start.27 = (bf16[16,2,4096]{2,0,1:T(8,128)(2,1)S(1)}, bf16[16,2,4096]{2,0,1:T(8,128)(2,1)S(1)}, u32[]{:S(2)}, u32[]{:S(2)}) collective-permute-start(bf16[16,2,4096]{2,0,1:T(8,128)(2,1)S(1)} %collective-permute-done.25), channel_id=1, source_target_pairs={{0,30},{2,0},{4,2},{6,4},{8,6},{10,8},{12,10},{14,12},{16,14},{18,... | collective-permute-start | bytes 786440 | tf_op jit(solution)/shard_map/ppermute | solution.py:60
  262.1 5.4 %collective-permute-done.26 = bf16[16,2,4096]{2,0,1:T(8,128)(2,1)S(1)} collective-permute-done((bf16[16,2,4096]{2,0,1:T(8,128)(2,1)S(1)}, bf16[16,2,4096]{2,0,1:T(8,128)(2,1)S(1)}, u32[]{:S(2)}, u32[]{:S(2)}) %collective-permute-start.26) | collective-permute-done | bytes 262176 | tf_op jit(solution)/shard_map/ppermute | solution.py:55
  267.9 5.8 %collective-permute-start.29 = (bf16[16,2,4096]{2,0,1:T(8,128)(2,1)S(1)}, bf16[16,2,4096]{2,0,1:T(8,128)(2,1)S(1)}, u32[]{:S(2)}, u32[]{:S(2)}) collective-permute-start(bf16[16,2,4096]{2,0,1:T(8,128)(2,1)S(1)} %collective-permute-done.27), channel_id=1, source_target_pairs={{0,30},{2,0},{4,2},{6,4},{8,6},{10,8},{12,10},{14,12},{16,14},{18,... | collective-permute-start | bytes 786440 | tf_op jit(solution)/shard_map/ppermute | solution.py:60
  273.7 4.6 %collective-permute-done.28 = bf16[16,2,4096]{2,0,1:T(8,128)(2,1)S(1)} collective-permute-done((bf16[16,2,4096]{2,0,1:T(8,128)(2,1)S(1)}, bf16[16,2,4096]{2,0,1:T(8,128)(2,1)S(1)}, u32[]{:S(2)}, u32[]{:S(2)}) %collective-permute-start.28) | collective-permute-done | bytes 262176 | tf_op jit(solution)/shard_map/ppermute | solution.py:55
  278.4 9.6 %collective-permute-done.30 = bf16[16,2,4096]{2,0,1:T(8,128)(2,1)S(1)} collective-permute-done((bf16[16,2,4096]{2,0,1:T(8,128)(2,1)S(1)}, bf16[16,2,4096]{2,0,1:T(8,128)(2,1)S(1)}, u32[]{:S(2)}, u32[]{:S(2)}) %collective-permute-start.30) | collective-permute-done | bytes 262176 | tf_op jit(solution)/shard_map/ppermute | solution.py:55
  288.1 1.2 fusion.30
  289.2 1.2 fusion.34
  290.5 3.4 fusion.8
  294.0 3.6 multiply_convert_fusion
  297.9 5.1 %add_convert_fusion = bf16[256,2,4096]{2,0,1:T(8,128)(2,1)} fusion(bf16[256,2,768]{2,0,1:T(8,128)(2,1)S(1)} %multiply_convert_fusion, bf16[1,768,4096]{2,1,0:T(8,128)(2,1)S(1)} %bitcast.129, f32[256,2]{0,1:T(2,128)S(1)} %fusion.42, f32[2,4096]{1,0:T(2,128)S(1)} %bitcast_convert_fusion), kind=kOutput, calls=%fused_computation | convolution fusion | flops 3227516928 | bytes 11307008 | tf_op jit(solution)/shard_map/rkf,fd->rkd/dot_general | solution.py:71
  305.1 6.3 %all-reduce = s32[8]{0:T(128)S(1)} all-reduce(s32[8]{0:T(128)S(1)} %dynamic-update-slice), channel_id=1, replica_groups=mesh['pop'=4,'tp'=16,'pp'=2] {'pop'}, use_global_device_ids=true, to_apply=%add | all-reduce | flops 8 | bytes 64
  311.5 7.2 %all-gather = bf16[4,2,14592]{2,1,0:T(2,128)(2,1)S(1)} all-gather(bf16[1,2,14592]{2,1,0:T(2,128)(2,1)S(1)} %bitcast.113), channel_id=1, replica_groups=mesh['pop'=4,'tp'=16,'pp'=2] {'pop'}, dimensions={0}, use_global_device_ids=true | all-gather | bytes 291840 | tf_op jit(solution)/shard_map/all_gather | solution.py:19
  319.1 4.4 %fusion.51 = bf16[4,768,1024]{2,1,0:T(8,128)(2,1)} fusion(bf16[4,2,768]{2,1,0:T(2,128)(2,1)S(1)} %reshape.60, bf16[4,2,1024]{2,1,0:T(2,128)(2,1)S(1)} %reshape.61), kind=kOutput, calls=%fused_computation.110 | convolution fusion | flops 12582912 | bytes 6320128 | tf_op jit(solution)/shard_map/gmi,gmj->gij/dot_general | solution.py:85
  323.6 4.5 %fusion.53 = bf16[4,1024,768]{2,1,0:T(8,128)(2,1)} fusion(bf16[4,2,1024]{2,1,0:T(2,128)(2,1)S(1)} %reshape.56, bf16[4,2,768]{2,1,0:T(2,128)(2,1)S(1)} %reshape.57), kind=kOutput, calls=%fused_computation.112 | convolution fusion | flops 12582912 | bytes 6320128 | tf_op jit(solution)/shard_map/gmi,gmj->gij/dot_general | solution.py:85
  328.1 4.5 %fusion.52 = bf16[4,1024,768]{2,1,0:T(8,128)(2,1)} fusion(bf16[4,2,1024]{2,1,0:T(2,128)(2,1)S(1)} %reshape.58, bf16[4,2,768]{2,1,0:T(2,128)(2,1)S(1)} %reshape.59), kind=kOutput, calls=%fused_computation.111 | convolution fusion | flops 12582912 | bytes 6320128 | tf_op jit(solution)/shard_map/gmi,gmj->gij/dot_general | solution.py:85
  332.6 6.0 %reduce_sum.58 = bf16[768,1024]{1,0:T(8,128)(2,1)} reduce(bf16[4,768,1024]{2,1,0:T(8,128)(2,1)} %fusion.51, bf16[]{:T(256)} %constant.152.clone.1), dimensions={0}, to_apply=%region_6.7 | reduce | flops 2359296 | bytes 7864322 | tf_op jit(solution)/shard_map/reduce_sum | solution.py:87
  338.7 5.3 %reduce_sum.56 = bf16[1024,768]{1,0:T(8,128)(2,1)} reduce(bf16[4,1024,768]{2,1,0:T(8,128)(2,1)} %fusion.53, bf16[]{:T(256)} %constant.152.clone.1), dimensions={0}, to_apply=%region_4.5 | reduce | flops 2359296 | bytes 7864322 | tf_op jit(solution)/shard_map/reduce_sum | solution.py:87
  344.0 5.5 %reduce_sum.57 = bf16[1024,768]{1,0:T(8,128)(2,1)} reduce(bf16[4,1024,768]{2,1,0:T(8,128)(2,1)} %fusion.52, bf16[]{:T(256)} %constant.152.clone.1), dimensions={0}, to_apply=%region_5.6 | reduce | flops 2359296 | bytes 7864322 | tf_op jit(solution)/shard_map/reduce_sum | solution.py:87
  349.5 29.1 %reduce-scatter.5.cloned.1.call-done = bf16[16,2,4096]{2,0,1:T(8,128)(2,1)} async-done(((bf16[256,2,4096]{2,0,1:T(8,128)(2,1)}), bf16[16,2,4096]{2,0,1:T(8,128)(2,1)}) %reduce-scatter.5.cloned.1.call-update) | async-done | bytes 262160 | tf_op jit(solution)/shard_map/reduce_scatter | solution.py:73
  378.6 1.1 fusion.29
  379.7 1.0 copy.19
  (142 shorter events, 13.6 us)
Async XLA Ops:
  7.2 4.0 %copy-start = (bf16[16,2,4096]{2,1,0:T(2,128)(2,1)S(1)}, bf16[16,2,4096]{2,1,0:T(2,128)(2,1)}, u32[]{:S(2)}) copy-start(bf16[16,2,4096]{2,1,0:T(2,128)(2,1)} %param.12) | copy-start | bytes 786436
  7.2 4.0 %copy-start.4 = (f32[1,4096]{1,0:T(1,128)S(1)}, f32[1,4096]{1,0:T(1,128)}, u32[]{:S(2)}) copy-start(f32[1,4096]{1,0:T(1,128)} %param.13) | copy-start | bytes 49156
  7.2 11.2 %copy-start.5 = (bf16[1,2,4096]{2,1,0:T(2,128)(2,1)S(1)}, bf16[1,2,4096]{2,1,0:T(2,128)(2,1)}, u32[]{:S(2)}) copy-start(bf16[1,2,4096]{2,1,0:T(2,128)(2,1)} %param.22) | copy-start | bytes 49156
  7.2 11.5 %copy-start.7 = (bf16[1,2,768]{2,1,0:T(2,128)(2,1)S(1)}, bf16[1,2,768]{2,1,0:T(2,128)(2,1)}, u32[]{:S(2)}) copy-start(bf16[1,2,768]{2,1,0:T(2,128)(2,1)} %param.20) | copy-start | bytes 9220
  7.2 11.5 %copy-start.6 = (bf16[1,2,768]{2,1,0:T(2,128)(2,1)S(1)}, bf16[1,2,768]{2,1,0:T(2,128)(2,1)}, u32[]{:S(2)}) copy-start(bf16[1,2,768]{2,1,0:T(2,128)(2,1)} %param.18) | copy-start | bytes 9220
  7.2 186.9 %reduce-scatter.3.cloned.1.call-start = ((), (), s32[]{:S(2)}) async-start(), calls=%async_computation.2 | async-start | bytes 4456448 | tf_op jit(solution)/shard_map/reduce_scatter | solution.py:73
  12.1 12.6 %collective-permute-start = (bf16[16,2,4096]{2,0,1:T(8,128)(2,1)S(1)}, bf16[16,2,4096]{2,0,1:T(8,128)(2,1)S(1)}, u32[]{:S(2)}, u32[]{:S(2)}) collective-permute-start(bf16[16,2,4096]{2,0,1:T(8,128)(2,1)S(1)} %get-tuple-element.15), channel_id=1, source_target_pairs={{0,2},{2,4},{4,6},{6,8},{8,10},{10,12},{12,14},{14,16},{16,18},{18... | collective-permute-start | bytes 786440 | tf_op jit(solution)/shard_map/ppermute | solution.py:55
  13.7 11.0 %collective-permute-start.1 = (bf16[16,2,4096]{2,0,1:T(8,128)(2,1)S(1)}, bf16[16,2,4096]{2,0,1:T(8,128)(2,1)S(1)}, u32[]{:S(2)}, u32[]{:S(2)}) collective-permute-start(bf16[16,2,4096]{2,0,1:T(8,128)(2,1)S(1)} %get-tuple-element.15), channel_id=1, source_target_pairs={{0,30},{2,0},{4,2},{6,4},{8,6},{10,8},{12,10},{14,12},{16,14},{18,... | collective-permute-start | bytes 786440 | tf_op jit(solution)/shard_map/ppermute | solution.py:60
  18.4 77.3 %copy-start.2 = (bf16[1,2,4096]{2,1,0:T(2,128)(2,1)S(1)}, bf16[1,2,4096]{2,1,0:T(2,128)(2,1)}, u32[]{:S(2)}) copy-start(bf16[1,2,4096]{2,1,0:T(2,128)(2,1)} %param.19) | copy-start | bytes 49156
  24.7 10.8 %collective-permute-start.2 = (bf16[16,2,4096]{2,0,1:T(8,128)(2,1)S(1)}, bf16[16,2,4096]{2,0,1:T(8,128)(2,1)S(1)}, u32[]{:S(2)}, u32[]{:S(2)}) collective-permute-start(bf16[16,2,4096]{2,0,1:T(8,128)(2,1)S(1)} %collective-permute-done), channel_id=1, source_target_pairs={{0,2},{2,4},{4,6},{6,8},{8,10},{10,12},{12,14},{14,16},{16,18},{18... | collective-permute-start | bytes 786440 | tf_op jit(solution)/shard_map/ppermute | solution.py:55
  24.7 10.8 %collective-permute-start.3 = (bf16[16,2,4096]{2,0,1:T(8,128)(2,1)S(1)}, bf16[16,2,4096]{2,0,1:T(8,128)(2,1)S(1)}, u32[]{:S(2)}, u32[]{:S(2)}) collective-permute-start(bf16[16,2,4096]{2,0,1:T(8,128)(2,1)S(1)} %collective-permute-done.1), channel_id=1, source_target_pairs={{0,30},{2,0},{4,2},{6,4},{8,6},{10,8},{12,10},{14,12},{16,14},{18,... | collective-permute-start | bytes 786440 | tf_op jit(solution)/shard_map/ppermute | solution.py:60
  35.5 9.9 %collective-permute-start.4 = (bf16[16,2,4096]{2,0,1:T(8,128)(2,1)S(1)}, bf16[16,2,4096]{2,0,1:T(8,128)(2,1)S(1)}, u32[]{:S(2)}, u32[]{:S(2)}) collective-permute-start(bf16[16,2,4096]{2,0,1:T(8,128)(2,1)S(1)} %collective-permute-done.2), channel_id=1, source_target_pairs={{0,2},{2,4},{4,6},{6,8},{8,10},{10,12},{12,14},{14,16},{16,18},{18... | collective-permute-start | bytes 786440 | tf_op jit(solution)/shard_map/ppermute | solution.py:55
  35.5 9.9 %collective-permute-start.5 = (bf16[16,2,4096]{2,0,1:T(8,128)(2,1)S(1)}, bf16[16,2,4096]{2,0,1:T(8,128)(2,1)S(1)}, u32[]{:S(2)}, u32[]{:S(2)}) collective-permute-start(bf16[16,2,4096]{2,0,1:T(8,128)(2,1)S(1)} %collective-permute-done.3), channel_id=1, source_target_pairs={{0,30},{2,0},{4,2},{6,4},{8,6},{10,8},{12,10},{14,12},{16,14},{18,... | collective-permute-start | bytes 786440 | tf_op jit(solution)/shard_map/ppermute | solution.py:60
  45.4 9.7 %collective-permute-start.6 = (bf16[16,2,4096]{2,0,1:T(8,128)(2,1)S(1)}, bf16[16,2,4096]{2,0,1:T(8,128)(2,1)S(1)}, u32[]{:S(2)}, u32[]{:S(2)}) collective-permute-start(bf16[16,2,4096]{2,0,1:T(8,128)(2,1)S(1)} %collective-permute-done.4), channel_id=1, source_target_pairs={{0,2},{2,4},{4,6},{6,8},{8,10},{10,12},{12,14},{14,16},{16,18},{18... | collective-permute-start | bytes 786440 | tf_op jit(solution)/shard_map/ppermute | solution.py:55
  45.4 9.7 %collective-permute-start.7 = (bf16[16,2,4096]{2,0,1:T(8,128)(2,1)S(1)}, bf16[16,2,4096]{2,0,1:T(8,128)(2,1)S(1)}, u32[]{:S(2)}, u32[]{:S(2)}) collective-permute-start(bf16[16,2,4096]{2,0,1:T(8,128)(2,1)S(1)} %collective-permute-done.5), channel_id=1, source_target_pairs={{0,30},{2,0},{4,2},{6,4},{8,6},{10,8},{12,10},{14,12},{16,14},{18,... | collective-permute-start | bytes 786440 | tf_op jit(solution)/shard_map/ppermute | solution.py:60
  55.1 9.7 %collective-permute-start.8 = (bf16[16,2,4096]{2,0,1:T(8,128)(2,1)S(1)}, bf16[16,2,4096]{2,0,1:T(8,128)(2,1)S(1)}, u32[]{:S(2)}, u32[]{:S(2)}) collective-permute-start(bf16[16,2,4096]{2,0,1:T(8,128)(2,1)S(1)} %collective-permute-done.6), channel_id=1, source_target_pairs={{0,2},{2,4},{4,6},{6,8},{8,10},{10,12},{12,14},{14,16},{16,18},{18... | collective-permute-start | bytes 786440 | tf_op jit(solution)/shard_map/ppermute | solution.py:55
  55.1 9.7 %collective-permute-start.9 = (bf16[16,2,4096]{2,0,1:T(8,128)(2,1)S(1)}, bf16[16,2,4096]{2,0,1:T(8,128)(2,1)S(1)}, u32[]{:S(2)}, u32[]{:S(2)}) collective-permute-start(bf16[16,2,4096]{2,0,1:T(8,128)(2,1)S(1)} %collective-permute-done.7), channel_id=1, source_target_pairs={{0,30},{2,0},{4,2},{6,4},{8,6},{10,8},{12,10},{14,12},{16,14},{18,... | collective-permute-start | bytes 786440 | tf_op jit(solution)/shard_map/ppermute | solution.py:60
  61.2 38.1 %copy-start.1 = (bf16[1,2,4096]{2,1,0:T(2,128)(2,1)S(1)}, bf16[1,2,4096]{2,1,0:T(2,128)(2,1)}, u32[]{:S(2)}) copy-start(bf16[1,2,4096]{2,1,0:T(2,128)(2,1)} %param.17) | copy-start | bytes 49156
  64.8 9.7 %collective-permute-start.10 = (bf16[16,2,4096]{2,0,1:T(8,128)(2,1)S(1)}, bf16[16,2,4096]{2,0,1:T(8,128)(2,1)S(1)}, u32[]{:S(2)}, u32[]{:S(2)}) collective-permute-start(bf16[16,2,4096]{2,0,1:T(8,128)(2,1)S(1)} %collective-permute-done.8), channel_id=1, source_target_pairs={{0,2},{2,4},{4,6},{6,8},{8,10},{10,12},{12,14},{14,16},{16,18},{18... | collective-permute-start | bytes 786440 | tf_op jit(solution)/shard_map/ppermute | solution.py:55
  64.8 9.7 %collective-permute-start.11 = (bf16[16,2,4096]{2,0,1:T(8,128)(2,1)S(1)}, bf16[16,2,4096]{2,0,1:T(8,128)(2,1)S(1)}, u32[]{:S(2)}, u32[]{:S(2)}) collective-permute-start(bf16[16,2,4096]{2,0,1:T(8,128)(2,1)S(1)} %collective-permute-done.9), channel_id=1, source_target_pairs={{0,30},{2,0},{4,2},{6,4},{8,6},{10,8},{12,10},{14,12},{16,14},{18,... | collective-permute-start | bytes 786440 | tf_op jit(solution)/shard_map/ppermute | solution.py:60
  70.9 32.0 %slice-start = ((s8[6291456]{0:T(1024)(128)(4,1)}), s8[4194304]{0:T(1024)(128)(4,1)S(1)}, s32[]{:S(2)}) async-start(s8[6291456]{0:T(1024)(128)(4,1)} %bitcast.118), calls=%async_computation.4 | async-start | bytes 8388608
  74.5 10.4 %collective-permute-start.12 = (bf16[16,2,4096]{2,0,1:T(8,128)(2,1)S(1)}, bf16[16,2,4096]{2,0,1:T(8,128)(2,1)S(1)}, u32[]{:S(2)}, u32[]{:S(2)}) collective-permute-start(bf16[16,2,4096]{2,0,1:T(8,128)(2,1)S(1)} %collective-permute-done.10), channel_id=1, source_target_pairs={{0,2},{2,4},{4,6},{6,8},{8,10},{10,12},{12,14},{14,16},{16,18},{18... | collective-permute-start | bytes 786440 | tf_op jit(solution)/shard_map/ppermute | solution.py:55
  74.5 11.5 %collective-permute-start.13 = (bf16[16,2,4096]{2,0,1:T(8,128)(2,1)S(1)}, bf16[16,2,4096]{2,0,1:T(8,128)(2,1)S(1)}, u32[]{:S(2)}, u32[]{:S(2)}) collective-permute-start(bf16[16,2,4096]{2,0,1:T(8,128)(2,1)S(1)} %collective-permute-done.11), channel_id=1, source_target_pairs={{0,30},{2,0},{4,2},{6,4},{8,6},{10,8},{12,10},{14,12},{16,14},{18,... | collective-permute-start | bytes 786440 | tf_op jit(solution)/shard_map/ppermute | solution.py:60
  84.9 10.1 %collective-permute-start.14 = (bf16[16,2,4096]{2,0,1:T(8,128)(2,1)S(1)}, bf16[16,2,4096]{2,0,1:T(8,128)(2,1)S(1)}, u32[]{:S(2)}, u32[]{:S(2)}) collective-permute-start(bf16[16,2,4096]{2,0,1:T(8,128)(2,1)S(1)} %collective-permute-done.12), channel_id=1, source_target_pairs={{0,2},{2,4},{4,6},{6,8},{8,10},{10,12},{12,14},{14,16},{16,18},{18... | collective-permute-start | bytes 786440 | tf_op jit(solution)/shard_map/ppermute | solution.py:55
  95.8 7.1 %slice-start.1 = ((s8[6291456]{0:T(1024)(128)(4,1)}), s8[2097152]{0:T(1024)(128)(4,1)S(1)}, s32[]{:S(2)}) async-start(s8[6291456]{0:T(1024)(128)(4,1)} %bitcast.118), calls=%async_computation.5 | async-start | bytes 4194304
  99.3 9.0 %slice-start.4 = ((s8[6291456]{0:T(1024)(128)(4,1)}), s8[4194304]{0:T(1024)(128)(4,1)S(1)}, s32[]{:S(2)}) async-start(s8[6291456]{0:T(1024)(128)(4,1)} %bitcast.122), calls=%async_computation.8 | async-start | bytes 8388608
  102.8 5.4 %slice-start.5 = ((s8[6291456]{0:T(1024)(128)(4,1)}), s8[2097152]{0:T(1024)(128)(4,1)S(1)}, s32[]{:S(2)}) async-start(s8[6291456]{0:T(1024)(128)(4,1)} %bitcast.122), calls=%async_computation.9 | async-start | bytes 4194304
  102.8 11.7 %slice-start.8 = ((s8[6291456]{0:T(1024)(128)(4,1)}), s8[4194304]{0:T(1024)(128)(4,1)S(1)}, s32[]{:S(2)}) async-start(s8[6291456]{0:T(1024)(128)(4,1)} %bitcast.126), calls=%async_computation.12 | async-start | bytes 8388608
  108.3 6.0 %copy-start.3 = (bf16[1,2,768]{2,1,0:T(2,128)(2,1)S(1)}, bf16[1,2,768]{2,1,0:T(2,128)(2,1)}, u32[]{:S(2)}) copy-start(bf16[1,2,768]{2,1,0:T(2,128)(2,1)} %param.21) | copy-start | bytes 9220
  108.3 6.3 %slice-start.9 = ((s8[6291456]{0:T(1024)(128)(4,1)}), s8[2097152]{0:T(1024)(128)(4,1)S(1)}, s32[]{:S(2)}) async-start(s8[6291456]{0:T(1024)(128)(4,1)} %bitcast.126), calls=%async_computation.13 | async-start | bytes 4194304
  119.7 258.9 %reduce-scatter.5.cloned.1.call-start = ((), (), s32[]{:S(2)}) async-start(), calls=%async_computation.3 | async-start | bytes 4456448 | tf_op jit(solution)/shard_map/reduce_scatter | solution.py:73
  195.2 7.3 %collective-permute-start.15 = (bf16[16,2,4096]{2,0,1:T(8,128)(2,1)S(1)}, bf16[16,2,4096]{2,0,1:T(8,128)(2,1)S(1)}, u32[]{:S(2)}, u32[]{:S(2)}) collective-permute-start(bf16[16,2,4096]{2,0,1:T(8,128)(2,1)S(1)} %fusion.23), channel_id=1, source_target_pairs={{0,1},{2,3},{4,5},{6,7},{8,9},{10,11},{12,13},{14,15},{16,17},{18,... | collective-permute-start | bytes 786440 | tf_op jit(solution)/shard_map/ppermute | solution.py:14
  203.4 9.8 %collective-permute-start.16 = (bf16[16,2,4096]{2,0,1:T(8,128)(2,1)S(1)}, bf16[16,2,4096]{2,0,1:T(8,128)(2,1)S(1)}, u32[]{:S(2)}, u32[]{:S(2)}) collective-permute-start(bf16[16,2,4096]{2,0,1:T(8,128)(2,1)S(1)} %get-tuple-element.13), channel_id=1, source_target_pairs={{0,2},{2,4},{4,6},{6,8},{8,10},{10,12},{12,14},{14,16},{16,18},{18... | collective-permute-start | bytes 786440 | tf_op jit(solution)/shard_map/ppermute | solution.py:55
  204.7 8.5 %collective-permute-start.17 = (bf16[16,2,4096]{2,0,1:T(8,128)(2,1)S(1)}, bf16[16,2,4096]{2,0,1:T(8,128)(2,1)S(1)}, u32[]{:S(2)}, u32[]{:S(2)}) collective-permute-start(bf16[16,2,4096]{2,0,1:T(8,128)(2,1)S(1)} %get-tuple-element.13), channel_id=1, source_target_pairs={{0,30},{2,0},{4,2},{6,4},{8,6},{10,8},{12,10},{14,12},{16,14},{18,... | collective-permute-start | bytes 786440 | tf_op jit(solution)/shard_map/ppermute | solution.py:60
  213.1 9.7 %collective-permute-start.18 = (bf16[16,2,4096]{2,0,1:T(8,128)(2,1)S(1)}, bf16[16,2,4096]{2,0,1:T(8,128)(2,1)S(1)}, u32[]{:S(2)}, u32[]{:S(2)}) collective-permute-start(bf16[16,2,4096]{2,0,1:T(8,128)(2,1)S(1)} %collective-permute-done.16), channel_id=1, source_target_pairs={{0,2},{2,4},{4,6},{6,8},{8,10},{10,12},{12,14},{14,16},{16,18},{18... | collective-permute-start | bytes 786440 | tf_op jit(solution)/shard_map/ppermute | solution.py:55
  213.2 9.7 %collective-permute-start.19 = (bf16[16,2,4096]{2,0,1:T(8,128)(2,1)S(1)}, bf16[16,2,4096]{2,0,1:T(8,128)(2,1)S(1)}, u32[]{:S(2)}, u32[]{:S(2)}) collective-permute-start(bf16[16,2,4096]{2,0,1:T(8,128)(2,1)S(1)} %collective-permute-done.17), channel_id=1, source_target_pairs={{0,30},{2,0},{4,2},{6,4},{8,6},{10,8},{12,10},{14,12},{16,14},{18,... | collective-permute-start | bytes 786440 | tf_op jit(solution)/shard_map/ppermute | solution.py:60
  222.8 9.9 %collective-permute-start.20 = (bf16[16,2,4096]{2,0,1:T(8,128)(2,1)S(1)}, bf16[16,2,4096]{2,0,1:T(8,128)(2,1)S(1)}, u32[]{:S(2)}, u32[]{:S(2)}) collective-permute-start(bf16[16,2,4096]{2,0,1:T(8,128)(2,1)S(1)} %collective-permute-done.18), channel_id=1, source_target_pairs={{0,2},{2,4},{4,6},{6,8},{8,10},{10,12},{12,14},{14,16},{16,18},{18... | collective-permute-start | bytes 786440 | tf_op jit(solution)/shard_map/ppermute | solution.py:55
  222.9 9.8 %collective-permute-start.21 = (bf16[16,2,4096]{2,0,1:T(8,128)(2,1)S(1)}, bf16[16,2,4096]{2,0,1:T(8,128)(2,1)S(1)}, u32[]{:S(2)}, u32[]{:S(2)}) collective-permute-start(bf16[16,2,4096]{2,0,1:T(8,128)(2,1)S(1)} %collective-permute-done.19), channel_id=1, source_target_pairs={{0,30},{2,0},{4,2},{6,4},{8,6},{10,8},{12,10},{14,12},{16,14},{18,... | collective-permute-start | bytes 786440 | tf_op jit(solution)/shard_map/ppermute | solution.py:60
  232.7 10.8 %collective-permute-start.22 = (bf16[16,2,4096]{2,0,1:T(8,128)(2,1)S(1)}, bf16[16,2,4096]{2,0,1:T(8,128)(2,1)S(1)}, u32[]{:S(2)}, u32[]{:S(2)}) collective-permute-start(bf16[16,2,4096]{2,0,1:T(8,128)(2,1)S(1)} %collective-permute-done.20), channel_id=1, source_target_pairs={{0,2},{2,4},{4,6},{6,8},{8,10},{10,12},{12,14},{14,16},{16,18},{18... | collective-permute-start | bytes 786440 | tf_op jit(solution)/shard_map/ppermute | solution.py:55
  232.7 11.1 %collective-permute-start.23 = (bf16[16,2,4096]{2,0,1:T(8,128)(2,1)S(1)}, bf16[16,2,4096]{2,0,1:T(8,128)(2,1)S(1)}, u32[]{:S(2)}, u32[]{:S(2)}) collective-permute-start(bf16[16,2,4096]{2,0,1:T(8,128)(2,1)S(1)} %collective-permute-done.21), channel_id=1, source_target_pairs={{0,30},{2,0},{4,2},{6,4},{8,6},{10,8},{12,10},{14,12},{16,14},{18,... | collective-permute-start | bytes 786440 | tf_op jit(solution)/shard_map/ppermute | solution.py:60
  243.5 12.3 %collective-permute-start.24 = (bf16[16,2,4096]{2,0,1:T(8,128)(2,1)S(1)}, bf16[16,2,4096]{2,0,1:T(8,128)(2,1)S(1)}, u32[]{:S(2)}, u32[]{:S(2)}) collective-permute-start(bf16[16,2,4096]{2,0,1:T(8,128)(2,1)S(1)} %collective-permute-done.22), channel_id=1, source_target_pairs={{0,2},{2,4},{4,6},{6,8},{8,10},{10,12},{12,14},{14,16},{16,18},{18... | collective-permute-start | bytes 786440 | tf_op jit(solution)/shard_map/ppermute | solution.py:55
  243.9 12.4 %collective-permute-start.25 = (bf16[16,2,4096]{2,0,1:T(8,128)(2,1)S(1)}, bf16[16,2,4096]{2,0,1:T(8,128)(2,1)S(1)}, u32[]{:S(2)}, u32[]{:S(2)}) collective-permute-start(bf16[16,2,4096]{2,0,1:T(8,128)(2,1)S(1)} %collective-permute-done.23), channel_id=1, source_target_pairs={{0,30},{2,0},{4,2},{6,4},{8,6},{10,8},{12,10},{14,12},{16,14},{18,... | collective-permute-start | bytes 786440 | tf_op jit(solution)/shard_map/ppermute | solution.py:60
  255.8 11.7 %collective-permute-start.26 = (bf16[16,2,4096]{2,0,1:T(8,128)(2,1)S(1)}, bf16[16,2,4096]{2,0,1:T(8,128)(2,1)S(1)}, u32[]{:S(2)}, u32[]{:S(2)}) collective-permute-start(bf16[16,2,4096]{2,0,1:T(8,128)(2,1)S(1)} %collective-permute-done.24), channel_id=1, source_target_pairs={{0,2},{2,4},{4,6},{6,8},{8,10},{10,12},{12,14},{14,16},{16,18},{18... | collective-permute-start | bytes 786440 | tf_op jit(solution)/shard_map/ppermute | solution.py:55
  255.8 34.7 %slice-start.2 = ((s8[6291456]{0:T(1024)(128)(4,1)}), s8[4194304]{0:T(1024)(128)(4,1)S(1)}, s32[]{:S(2)}) async-start(s8[6291456]{0:T(1024)(128)(4,1)} %bitcast.120), calls=%async_computation.6 | async-start | bytes 8388608
  256.3 11.6 %collective-permute-start.27 = (bf16[16,2,4096]{2,0,1:T(8,128)(2,1)S(1)}, bf16[16,2,4096]{2,0,1:T(8,128)(2,1)S(1)}, u32[]{:S(2)}, u32[]{:S(2)}) collective-permute-start(bf16[16,2,4096]{2,0,1:T(8,128)(2,1)S(1)} %collective-permute-done.25), channel_id=1, source_target_pairs={{0,30},{2,0},{4,2},{6,4},{8,6},{10,8},{12,10},{14,12},{16,14},{18,... | collective-permute-start | bytes 786440 | tf_op jit(solution)/shard_map/ppermute | solution.py:60
  267.5 10.9 %collective-permute-start.28 = (bf16[16,2,4096]{2,0,1:T(8,128)(2,1)S(1)}, bf16[16,2,4096]{2,0,1:T(8,128)(2,1)S(1)}, u32[]{:S(2)}, u32[]{:S(2)}) collective-permute-start(bf16[16,2,4096]{2,0,1:T(8,128)(2,1)S(1)} %collective-permute-done.26), channel_id=1, source_target_pairs={{0,2},{2,4},{4,6},{6,8},{8,10},{10,12},{12,14},{14,16},{16,18},{18... | collective-permute-start | bytes 786440 | tf_op jit(solution)/shard_map/ppermute | solution.py:55
  267.9 10.5 %collective-permute-start.29 = (bf16[16,2,4096]{2,0,1:T(8,128)(2,1)S(1)}, bf16[16,2,4096]{2,0,1:T(8,128)(2,1)S(1)}, u32[]{:S(2)}, u32[]{:S(2)}) collective-permute-start(bf16[16,2,4096]{2,0,1:T(8,128)(2,1)S(1)} %collective-permute-done.27), channel_id=1, source_target_pairs={{0,30},{2,0},{4,2},{6,4},{8,6},{10,8},{12,10},{14,12},{16,14},{18,... | collective-permute-start | bytes 786440 | tf_op jit(solution)/shard_map/ppermute | solution.py:60
  278.3 9.7 %collective-permute-start.30 = (bf16[16,2,4096]{2,0,1:T(8,128)(2,1)S(1)}, bf16[16,2,4096]{2,0,1:T(8,128)(2,1)S(1)}, u32[]{:S(2)}, u32[]{:S(2)}) collective-permute-start(bf16[16,2,4096]{2,0,1:T(8,128)(2,1)S(1)} %collective-permute-done.28), channel_id=1, source_target_pairs={{0,2},{2,4},{4,6},{6,8},{8,10},{10,12},{12,14},{14,16},{16,18},{18... | collective-permute-start | bytes 786440 | tf_op jit(solution)/shard_map/ppermute | solution.py:55
  288.0 2.4 slice-start.3
  289.2 4.7 %slice-start.6 = ((s8[6291456]{0:T(1024)(128)(4,1)}), s8[4194304]{0:T(1024)(128)(4,1)S(1)}, s32[]{:S(2)}) async-start(s8[6291456]{0:T(1024)(128)(4,1)} %bitcast.124), calls=%async_computation.10 | async-start | bytes 8388608
  290.4 3.5 slice-start.7
  290.5 7.4 %slice-start.10 = ((s8[6291456]{0:T(1024)(128)(4,1)}), s8[4194304]{0:T(1024)(128)(4,1)S(1)}, s32[]{:S(2)}) async-start(s8[6291456]{0:T(1024)(128)(4,1)} %bitcast.128), calls=%async_computation.14 | async-start | bytes 8388608
  293.9 3.9 %slice-start.11 = ((s8[6291456]{0:T(1024)(128)(4,1)}), s8[2097152]{0:T(1024)(128)(4,1)S(1)}, s32[]{:S(2)}) async-start(s8[6291456]{0:T(1024)(128)(4,1)} %bitcast.128), calls=%async_computation.15 | async-start | bytes 4194304
  303.0 0.7 copy-start.9
  303.0 1.9 copy-start.8
Sparse Core Ops, SparseCore 0:
  119.8 74.2 reduce-scatter.2
  303.1 75.4 reduce-scatter.4
